TPU v7x, 128 devices: a whole 4x4x4 slice. The times are simulated.
128 devices in a mesh: rows: 4 (over z_lo, core), cols: 32 (over y, x, z_hi).
Axes of the slice: x: 4, y: 4, z: 4 (z_hi: 2, z_lo: 2; z = z_hi * 2 + z_lo), core: 2. Of those that a mesh axis runs over, the one named last changes fastest.
Arguments:
- pair_integrals: float32 [4096, 16384], P('rows', 'cols'), may hold values from -6 to 6
- left_factor: float32 [4096, 1024], P('rows', 'cols'), may hold values from -0.9375 to 0.9375
- core: float32 [1024, 1024], replicated, may hold values from -6 to 6
- right_factor: float32 [16384, 1024], P('cols', 'rows'), may hold values from -0.46875 to 0.46875
Outputs:
- core_next: float32 [1024, 1024], replicated
All inputs are finite; a program needn't handle non-finite values.
Results may differ from a plain program's by a relative error of at most 0.000062.
Values sent between devices are 32-bit elements; how exact they have to be, the bound alone decides.
A program may use at most 128 MiB of HBM per device.

v0:
```python
import functools
import jax
import jax.numpy as jnp
from jax import lax
from jax.sharding import Mesh
from jax.sharding import PartitionSpec as P

COLS = ("cols_0", "cols_1", "cols_2")
ROWS = ("rows_0", "rows_1")
ROWS_COLS = ("rows_0", "rows_1", "cols_0", "cols_1", "cols_2")


def joined_along(parts, dim):
    shape = list(parts.shape[1:])
    shape[dim] *= parts.shape[0]
    return jnp.moveaxis(parts, 0, dim).reshape(shape)


def copy_for_each(x, axis):
    devices = lax.axis_size(axis)
    return lax.all_to_all(jnp.broadcast_to(x[None], (devices, *x.shape)), axis, 0, 0, tiled=True)


def gathered_copies(x, axis, dim):
    return joined_along(copy_for_each(x, axis), dim)


def one_axis_at_a_time(x, axes):
    return functools.reduce(lax.psum, axes, x)


def product(left, right):
    return jnp.dot(left, right, precision=lax.Precision.HIGHEST, preferred_element_type=jnp.float32)


def shards(pair_integrals, left_factor, core, right_factor):
    left_rows = lax.all_gather(left_factor, COLS, axis=1, tiled=True)
    right_rows = gathered_copies(right_factor, ROWS, 1)
    mixed = product(core, right_rows.T)
    residual = pair_integrals - product(left_rows, mixed)
    along = product(residual, right_rows)
    local_term = product(left_rows.T, along)
    gradient = lax.psum(local_term, ROWS_COLS)
    numer = jnp.sum(gradient * gradient)
    image = product(left_rows, product(gradient, right_rows.T))
    denom = one_axis_at_a_time(jnp.sum(image * image), ROWS_COLS)
    return core + numer / denom * gradient


def solution(mesh):
    finer = Mesh(
        mesh.devices.reshape(2, 2, 4, 4, 2), ("rows_0", "rows_1", "cols_0", "cols_1", "cols_2")
    )
    placed = (P(ROWS, COLS), P(ROWS, COLS), P(), P(COLS, ROWS))
    return jax.shard_map(shards, mesh=finer, in_specs=placed, out_specs=P(), check_vma=False)
```

profile of v0, /device:TPU:0, one launch (start us, length us, event | category | flops | bytes accessed | tf_op | source)
XLA Modules:
  0.0 376.6 jit_solution(10287196216406322099)
XLA Ops:
  6.5 0.0 all-gather.2.cloned.1.call-start
  6.5 0.7 all-gather.2.cloned.1.call-update
  7.3 0.0 all-reduce.2.cloned.1.call-start
  7.3 1.2 copy.7
  8.5 0.0 copy-start
  8.6 0.3 broadcast_in_dim.2
  8.8 30.0 %all_to_all.5 = f32[4,512,256]{1,2,0:T(8,128)S(1)} all-to-all(f32[4,512,256]{1,2,0:T(8,128)S(1)} %broadcast_in_dim.2), channel_id=1, replica_groups=mesh['rows_0'=2,'rows_1'=2,'cols_0'=4,'cols_1'=4,'cols_2'=2] {'rows_0','..., dimensions={0} | all-to-all | bytes 4194304 | tf_op jit(solution)/shard_map/all_to_all | solution.py:21
  38.8 0.0 copy-done
  38.8 8.0 %fusion.1 = f32[1024,512]{1,0:T(8,128)} fusion(f32[1024,1024]{1,0:T(8,128)S(1)} %copy-done, f32[512,1024]{0,1:T(8,128)S(1)} %bitcast.19), kind=kOutput, calls=%fused_computation.6 | convolution fusion | flops 6442450944 | bytes 8388608 | tf_op jit(solution)/shard_map/dot_general | solution.py:33
  46.8 48.8 %all-gather.2.cloned.1.call-done = f32[1024,1024]{0,1:T(8,128)} async-done(((f32[1024,32]{0,1:T(8,128)}), f32[1024,1024]{0,1:T(8,128)}) %all-gather.2.cloned.1.call-update) | async-done | bytes 4194320 | tf_op jit(solution)/shard_map/all_gather | solution.py:37
  95.6 0.0 copy-start.3
  95.6 9.9 %fusion.2 = f32[512,1024]{0,1:T(8,128)S(1)} fusion(f32[1024,512]{1,0:T(8,128)} %fusion.1, f32[1024,1024]{0,1:T(8,128)} %all-gather.2.cloned.1.call-done), kind=kOutput, calls=%fused_computation.7 | convolution fusion | flops 6442450944 | bytes 8388608 | tf_op jit(solution)/shard_map/dot_general | solution.py:33
  105.6 0.0 copy-done.3
  105.6 0.0 copy-start.1
  105.6 6.9 %fusion = f32[1024,1024]{1,0:T(8,128)S(1)} fusion(f32[512,1024]{0,1:T(8,128)S(1)} %bitcast.20, f32[1024,512]{1,0:T(8,128)S(1)} %copy-done.3, f32[512,1024]{0,1:T(8,128)S(1)} %fusion.2), kind=kOutput, calls=%fused_computation.4 | convolution fusion | flops 6442975232 | bytes 10485760 | tf_op jit(solution)/shard_map/dot_general | solution.py:33
  112.5 0.0 copy-done.1
  112.5 29.8 %convolution_bitcast_fusion = f32[1024,1024]{0,1:T(8,128)} fusion(f32[1024,1024]{1,0:T(8,128)S(1)} %fusion, f32[1024,1024]{0,1:T(8,128)S(1)} %copy-done.1), kind=kOutput, calls=%fused_computation.2 | convolution fusion | flops 12884901888 | bytes 12582912 | tf_op jit(solution)/shard_map/dot_general | solution.py:33
  142.3 0.0 all-reduce.2.cloned.1.call-update
  142.3 150.9 %all-reduce.2.cloned.1.call-done = f32[1024,1024]{0,1:T(8,128)} async-done(((f32[1024,1024]{0,1:T(8,128)}), f32[1024,1024]{0,1:T(8,128)}) %all-reduce.2.cloned.1.call-update) | async-done | bytes 4194320 | tf_op jit(solution)/shard_map/psum | solution.py:43
  293.2 0.0 copy-start.2
  293.2 8.8 %fusion.3 = f32[1024,512]{1,0:T(8,128)S(1)} fusion(f32[1024,1024]{0,1:T(8,128)} %all-reduce.2.cloned.1.call-done, f32[512,1024]{0,1:T(8,128)S(1)} %bitcast.21), kind=kOutput, calls=%fused_computation.8 | convolution fusion | flops 6442450944 | bytes 8388608 | tf_op jit(solution)/shard_map/dot_general | solution.py:33
  302.0 0.0 copy-done.2
  302.0 7.8 %multiply_reduce_fusion.1 = f32[]{:T(128)} fusion(f32[1024,512]{1,0:T(8,128)S(1)} %fusion.3, f32[1024,1024]{0,1:T(8,128)S(1)} %copy-done.2), kind=kOutput, calls=%fused_computation.5 | convolution fusion | flops 6443499520 | bytes 6291460 | tf_op jit(solution)/shard_map/dot_general | solution.py:33
  309.8 5.5 %psum.43 = f32[]{:T(128)} all-reduce(f32[]{:T(128)} %multiply_reduce_fusion.1), channel_id=1, replica_groups=mesh['rows_0'=2,'rows_1'=2,'cols_0'=4,'cols_1'=4,'cols_2'=2] {'rows_0'}, use_global_device_ids=true, to_apply=%region_3.0 | all-reduce | flops 1 | bytes 8 | tf_op jit(solution)/shard_map/psum | solution.py:29
  315.4 3.1 psum.44
  318.4 10.2 %psum.45 = f32[]{:T(128)} all-reduce(f32[]{:T(128)} %psum.44), channel_id=1, replica_groups=mesh['rows_0'=2,'rows_1'=2,'cols_0'=4,'cols_1'=4,'cols_2'=2] {'cols_0'}, use_global_device_ids=true, to_apply=%region_5.0 | all-reduce | flops 1 | bytes 8 | tf_op jit(solution)/shard_map/psum | solution.py:29
  328.7 11.1 %psum.46 = f32[]{:T(128)} all-reduce(f32[]{:T(128)} %psum.45), channel_id=1, replica_groups=mesh['rows_0'=2,'rows_1'=2,'cols_0'=4,'cols_1'=4,'cols_2'=2] {'cols_1'}, use_global_device_ids=true, to_apply=%region_6.0 | all-reduce | flops 1 | bytes 8 | tf_op jit(solution)/shard_map/psum | solution.py:29
  339.8 5.3 %copy.8 = f32[1024,1024]{0,1:T(8,128)} copy(f32[1024,1024]{1,0:T(8,128)} %param.6) | data formatting | bytes 8388608 | tf_op args[2]
  345.1 7.1 %psum.47 = f32[]{:T(128)} all-reduce(f32[]{:T(128)} %psum.46), channel_id=1, replica_groups=mesh['rows_0'=2,'rows_1'=2,'cols_0'=4,'cols_1'=4,'cols_2'=2] {'cols_2'}, use_global_device_ids=true, to_apply=%region_7.0 | all-reduce | flops 1 | bytes 8 | tf_op jit(solution)/shard_map/psum | solution.py:29
  352.2 3.9 %multiply_reduce_fusion = f32[]{:T(128)} fusion(f32[1024,1024]{0,1:T(8,128)} %all-reduce.2.cloned.1.call-done), kind=kLoop, calls=%fused_computation.1 | loop fusion | flops 2097151 | bytes 4194308 | tf_op jit(solution)/shard_map/reduce_sum | solution.py:44
  357.3 6.9 %multiply_add_fusion = f32[1024,1024]{0,1:T(8,128)} fusion(f32[1024,1024]{0,1:T(8,128)} %copy.8, f32[1024,1024]{0,1:T(8,128)} %all-reduce.2.cloned.1.call-done, f32[]{:T(128)S(6)} %div.3), kind=kLoop, calls=%fused_computation | loop fusion | flops 2097152 | bytes 12582916 | tf_op jit(solution)/shard_map/add | solution.py:47
  364.2 5.3 %copy.9 = f32[1024,1024]{1,0:T(8,128)} copy(f32[1024,1024]{0,1:T(8,128)} %multiply_add_fusion) | data formatting | bytes 8388608 | tf_op jit(solution)/shard_map/add | solution.py:47
Async XLA Ops:
  6.5 89.1 %all-gather.2.cloned.1.call-start = ((), (), s32[]{:S(2)}) async-start(), calls=%async_computation.1 | async-start | bytes 4325376 | tf_op jit(solution)/shard_map/all_gather | solution.py:37
  7.3 286.0 %all-reduce.2.cloned.1.call-start = ((), (), s32[]{:S(2)}) async-start(), calls=%async_computation.2 | async-start | bytes 8388608 | tf_op jit(solution)/shard_map/psum | solution.py:43
  8.5 30.2 %copy-start = (f32[1024,1024]{1,0:T(8,128)S(1)}, f32[1024,1024]{1,0:T(8,128)}, u32[]{:S(2)}) copy-start(f32[1024,1024]{1,0:T(8,128)} %param.6) | copy-start | bytes 12582916
  95.6 9.9 %copy-start.3 = (f32[1024,512]{1,0:T(8,128)S(1)}, f32[1024,512]{1,0:T(8,128)}, u32[]{:S(2)}) copy-start(f32[1024,512]{1,0:T(8,128)} %param.4) | copy-start | bytes 6291460
  105.6 6.9 %copy-start.1 = (f32[1024,1024]{0,1:T(8,128)S(1)}, f32[1024,1024]{0,1:T(8,128)}, u32[]{:S(2)}) copy-start(f32[1024,1024]{0,1:T(8,128)} %all-gather.2.cloned.1.call-done) | copy-start | bytes 12582916
  293.2 8.8 %copy-start.2 = (f32[1024,1024]{0,1:T(8,128)S(1)}, f32[1024,1024]{0,1:T(8,128)}, u32[]{:S(2)}) copy-start(f32[1024,1024]{0,1:T(8,128)} %all-gather.2.cloned.1.call-done) | copy-start | bytes 12582916
Sparse Core Ops, SparseCore 0:
  10.3 85.2 all-gather.1
  142.4 150.7 all-reduce.1
where the time goes:
time: 384 us; the launch traced here: 377 us
  waiting for transfers between devices  201 us (52%)
  matrix products  71.1 us (19%)
  blocking collectives  67 us (17%)
  between operations  15 us (4%)
  local copies, waits for them, and re-layouts  12.2 us (3%)
  other arithmetic  10.7 us (3%)
    psum x1, waiting for transfers between devices, shards(): gradient = lax.psum(local_term, ROWS_COLS)  151 us
    dot_general x6, matrix products, product(): jnp.dot(left, right, precision=lax.Precision.HIGHEST, preferred_element_t...  71.1 us
    all_gather x1, waiting for transfers between devices, shards(): left_rows = lax.all_gather(left_factor, COLS, axis=1, tiled=True)  48.8 us
    psum x5, blocking collectives, one_axis_at_a_time(): return functools.reduce(lax.psum, axes, x)  37.1 us
    all_to_all x1, blocking collectives, copy_for_each(): lax.all_to_all(jnp.broadcast_to(x[None], (devices, *x.shape)), axis, 0, 0...  30 us
  transfers between devices with their start and end apart: 2, of which 2 were waited for; matrix products, arithmetic and copies ran while one was open for 3% of the time, Pallas kernels for 0%

commit v1 on v0

--- a/solution.py
+++ b/solution.py
@@ -34,7 +34,9 @@
 
 
 def shards(pair_integrals, left_factor, core, right_factor):
-    left_rows = lax.all_gather(left_factor, COLS, axis=1, tiled=True)
+    left_rows = jnp.concatenate(
+        lax.all_to_all(jnp.stack([left_factor] * lax.axis_size(COLS)), COLS, 0, 0), axis=1
+    )
     right_rows = gathered_copies(right_factor, ROWS, 1)
     mixed = product(core, right_rows.T)
     residual = pair_integrals - product(left_rows, mixed)

time: 384 us -> 403 us (1.049)
  starting transfers between devices: 0.04 us -> 10.5 us
  matrix products: 71.1 us -> 76.3 us
    all_to_all x0 -> x1, waiting for transfers between devices: none -> 50.7 us  [shards(): lax.all_to_all(jnp.stack([left_factor] * lax.axis_size(COLS)), COLS, 0, 0)]
    all_gather x1 -> x0, waiting for transfers between devices: 48.8 us -> none  [shards(): left_rows = lax.all_gather(left_factor, COLS, axis=1, tiled=True)]
    all_to_all x0 -> x1, starting transfers between devices: none -> 10.5 us  [shards(): lax.all_to_all(jnp.stack([left_factor] * lax.axis_size(COLS)), COLS, 0, 0)]
    dot_general x6, matrix products: 71.1 us -> 76.3 us  [product(): jnp.dot(left, right, precision=lax.Precision.HIGHEST, preferred_element_t...]
  transfers between devices with their start and end apart: 2 -> 2, of which waited for: 2 -> 2; matrix products, arithmetic and copies ran while one was open for 3% -> 2% of each run, Pallas kernels for 0% -> 0%
where the time goes in v1:
time: 403 us; the launch traced here: 396 us
  waiting for transfers between devices  203 us (50%)
  matrix products  76.3 us (19%)
  blocking collectives  65.8 us (16%)
  between operations  15 us (4%)
  local copies, waits for them, and re-layouts  14.8 us (4%)
  other arithmetic  10.7 us (3%)
  starting transfers between devices  10.5 us (3%)
    psum x1, waiting for transfers between devices, shards(): gradient = lax.psum(local_term, ROWS_COLS)  152 us
    dot_general x6, matrix products, product(): jnp.dot(left, right, precision=lax.Precision.HIGHEST, preferred_element_t...  76.3 us
    all_to_all x1, waiting for transfers between devices, shards(): lax.all_to_all(jnp.stack([left_factor] * lax.axis_size(COLS)), COLS, 0, 0)  50.7 us
    psum x5, blocking collectives, one_axis_at_a_time(): return functools.reduce(lax.psum, axes, x)  37.1 us
    all_to_all x1, blocking collectives, copy_for_each(): lax.all_to_all(jnp.broadcast_to(x[None], (devices, *x.shape)), axis, 0, 0...  28.8 us
    all_to_all x1, starting transfers between devices, shards(): lax.all_to_all(jnp.stack([left_factor] * lax.axis_size(COLS)), COLS, 0, 0)  10.5 us
  transfers between devices with their start and end apart: 2, of which 2 were waited for; matrix products, arithmetic and copies ran while one was open for 2% of the time, Pallas kernels for 0%

profile of v1, /device:TPU:0, one launch (start us, length us, event | category | flops | bytes accessed | tf_op | source)
XLA Modules:
  0.0 396.3 jit_solution(2036621160203371787)
XLA Ops:
  6.5 0.0 copy-start.1
  6.5 1.3 copy.8
  7.8 0.3 broadcast_in_dim.2
  8.1 28.8 %all_to_all.10 = f32[4,512,256]{1,2,0:T(8,128)S(1)} all-to-all(f32[4,512,256]{1,2,0:T(8,128)S(1)} %broadcast_in_dim.2), channel_id=1, replica_groups=mesh['rows_0'=2,'rows_1'=2,'cols_0'=4,'cols_1'=4,'cols_2'=2] {'rows_0','..., dimensions={0} | all-to-all | bytes 4194304 | tf_op jit(solution)/shard_map/all_to_all | solution.py:21
  36.9 0.0 copy-done.1
  36.9 2.5 stack.2
  39.4 10.5 %all-to-all-start.1 = ((f32[32,1024,32]{1,2,0:T(8,128)}), f32[32,1024,32]{1,2,0:T(8,128)}, u32[]{:S(2)}, u32[]{:S(2)}) async-start(f32[32,1024,32]{1,2,0:T(8,128)} %stack.2), calls=%async_computation.1 | async-start | bytes 8388608 | tf_op jit(solution)/shard_map/all_to_all | solution.py:38
  49.9 0.0 all-reduce.2.cloned.1.call-start
  49.9 9.7 %fusion.1 = f32[1024,512]{1,0:T(8,128)} fusion(f32[1024,1024]{1,0:T(8,128)} %param.6, f32[512,1024]{0,1:T(8,128)S(1)} %bitcast.22), kind=kOutput, calls=%fused_computation.6 | convolution fusion | flops 6442450944 | bytes 8388608 | tf_op jit(solution)/shard_map/dot_general | solution.py:33
  59.6 50.7 %all-to-all-done.1 = f32[32,1024,32]{1,2,0:T(8,128)} async-done(((f32[32,1024,32]{1,2,0:T(8,128)}), f32[32,1024,32]{1,2,0:T(8,128)}, u32[]{:S(2)}, u32[]{:S(2)}) %all-to-all-start.1) | async-done | bytes 4194336 | tf_op jit(solution)/shard_map/all_to_all | solution.py:38
  110.3 0.0 copy-start
  110.3 9.9 %fusion.2 = f32[512,1024]{0,1:T(8,128)S(1)} fusion(f32[1024,512]{1,0:T(8,128)} %fusion.1, f32[1024,1024]{0,1:T(8,128)} %bitcast.3), kind=kOutput, calls=%fused_computation.7 | convolution fusion | flops 6442450944 | bytes 8388608 | tf_op jit(solution)/shard_map/dot_general | solution.py:33
  120.2 0.0 copy-done
  120.2 6.9 %fusion = f32[1024,1024]{1,0:T(8,128)S(1)} fusion(f32[512,1024]{0,1:T(8,128)S(1)} %bitcast.23, f32[1024,512]{1,0:T(8,128)S(1)} %copy-done, f32[512,1024]{0,1:T(8,128)S(1)} %fusion.2), kind=kOutput, calls=%fused_computation.4 | convolution fusion | flops 6442975232 | bytes 10485760 | tf_op jit(solution)/shard_map/dot_general | solution.py:33
  127.1 31.5 %convolution_bitcast_fusion = f32[1024,1024]{0,1:T(8,128)} fusion(f32[1024,1024]{1,0:T(8,128)S(1)} %fusion, f32[1024,1024]{0,1:T(8,128)} %bitcast.3), kind=kOutput, calls=%fused_computation.2 | convolution fusion | flops 12884901888 | bytes 12582912 | tf_op jit(solution)/shard_map/dot_general | solution.py:33
  158.6 0.0 all-reduce.2.cloned.1.call-update
  158.7 152.4 %all-reduce.2.cloned.1.call-done = f32[1024,1024]{0,1:T(8,128)} async-done(((f32[1024,1024]{0,1:T(8,128)}), f32[1024,1024]{0,1:T(8,128)}) %all-reduce.2.cloned.1.call-update) | async-done | bytes 4194320 | tf_op jit(solution)/shard_map/psum | solution.py:45
  311.1 8.6 %fusion.3 = f32[1024,512]{1,0:T(8,128)S(1)} fusion(f32[1024,1024]{0,1:T(8,128)} %all-reduce.2.cloned.1.call-done, f32[512,1024]{0,1:T(8,128)S(1)} %bitcast.24), kind=kOutput, calls=%fused_computation.8 | convolution fusion | flops 6442450944 | bytes 8388608 | tf_op jit(solution)/shard_map/dot_general | solution.py:33
  319.7 9.7 %multiply_reduce_fusion.1 = f32[]{:T(128)} fusion(f32[1024,512]{1,0:T(8,128)S(1)} %fusion.3, f32[1024,1024]{0,1:T(8,128)} %bitcast.3), kind=kOutput, calls=%fused_computation.5 | convolution fusion | flops 6443499520 | bytes 6291460 | tf_op jit(solution)/shard_map/dot_general | solution.py:33
  329.4 5.5 %psum.43 = f32[]{:T(128)} all-reduce(f32[]{:T(128)} %multiply_reduce_fusion.1), channel_id=1, replica_groups=mesh['rows_0'=2,'rows_1'=2,'cols_0'=4,'cols_1'=4,'cols_2'=2] {'rows_0'}, use_global_device_ids=true, to_apply=%region_3.0 | all-reduce | flops 1 | bytes 8 | tf_op jit(solution)/shard_map/psum | solution.py:29
  335.0 3.1 psum.44
  338.1 10.2 %psum.45 = f32[]{:T(128)} all-reduce(f32[]{:T(128)} %psum.44), channel_id=1, replica_groups=mesh['rows_0'=2,'rows_1'=2,'cols_0'=4,'cols_1'=4,'cols_2'=2] {'cols_0'}, use_global_device_ids=true, to_apply=%region_5.0 | all-reduce | flops 1 | bytes 8 | tf_op jit(solution)/shard_map/psum | solution.py:29
  348.3 11.1 %psum.46 = f32[]{:T(128)} all-reduce(f32[]{:T(128)} %psum.45), channel_id=1, replica_groups=mesh['rows_0'=2,'rows_1'=2,'cols_0'=4,'cols_1'=4,'cols_2'=2] {'cols_1'}, use_global_device_ids=true, to_apply=%region_6.0 | all-reduce | flops 1 | bytes 8 | tf_op jit(solution)/shard_map/psum | solution.py:29
  359.4 5.3 %copy.9 = f32[1024,1024]{0,1:T(8,128)} copy(f32[1024,1024]{1,0:T(8,128)} %param.6) | data formatting | bytes 8388608 | tf_op args[2]
  364.8 7.1 %psum.47 = f32[]{:T(128)} all-reduce(f32[]{:T(128)} %psum.46), channel_id=1, replica_groups=mesh['rows_0'=2,'rows_1'=2,'cols_0'=4,'cols_1'=4,'cols_2'=2] {'cols_2'}, use_global_device_ids=true, to_apply=%region_7.0 | all-reduce | flops 1 | bytes 8 | tf_op jit(solution)/shard_map/psum | solution.py:29
  371.8 3.9 multiply_reduce_fusion
  377.0 6.9 %multiply_add_fusion = f32[1024,1024]{0,1:T(8,128)} fusion(f32[1024,1024]{0,1:T(8,128)} %copy.9, f32[1024,1024]{0,1:T(8,128)} %all-reduce.2.cloned.1.call-done, f32[]{:T(128)S(6)} %div.3), kind=kLoop, calls=%fused_computation | loop fusion | flops 2097152 | bytes 12582916 | tf_op jit(solution)/shard_map/add | solution.py:49
  383.9 5.3 %copy.10 = f32[1024,1024]{1,0:T(8,128)} copy(f32[1024,1024]{0,1:T(8,128)} %multiply_add_fusion) | data formatting | bytes 8388608 | tf_op jit(solution)/shard_map/add | solution.py:49
Async XLA Ops:
  6.5 30.3 %copy-start.1 = (f32[1024,32]{0,1:T(8,128)S(1)}, f32[1024,32]{0,1:T(8,128)}, u32[]{:S(2)}) copy-start(f32[1024,32]{0,1:T(8,128)} %param.5) | copy-start | bytes 393220
  39.4 70.9 %all-to-all-start.1 = ((f32[32,1024,32]{1,2,0:T(8,128)}), f32[32,1024,32]{1,2,0:T(8,128)}, u32[]{:S(2)}, u32[]{:S(2)}) async-start(f32[32,1024,32]{1,2,0:T(8,128)} %stack.2), calls=%async_computation.1 | async-start | bytes 8388608 | tf_op jit(solution)/shard_map/all_to_all | solution.py:38
  49.9 261.2 %all-reduce.2.cloned.1.call-start = ((), (), s32[]{:S(2)}) async-start(), calls=%async_computation.2 | async-start | bytes 8388608 | tf_op jit(solution)/shard_map/psum | solution.py:45
  110.3 9.9 %copy-start = (f32[1024,512]{1,0:T(8,128)S(1)}, f32[1024,512]{1,0:T(8,128)}, u32[]{:S(2)}) copy-start(f32[1024,512]{1,0:T(8,128)} %param.4) | copy-start | bytes 6291460
Sparse Core Ops, SparseCore 0:
  158.8 152.2 all-reduce.1
